TPU v7x, 32 devices: a whole 2x2x4 slice. The times are simulated.
32 devices in a mesh: cell: 8 (over z, y), gene: 4 (over x, core).
Axes of the slice: x: 2, y: 2, z: 4, core: 2. Of those that a mesh axis runs over, the one named last changes fastest.
Arguments:
- counts: int32 [8192, 16384], P('cell', 'gene'), may hold values from 0 to 4
- factors: float32 [8192, 64], P(('cell', 'gene')), may hold values from -1.5 to 1.5
- loadings: float32 [16384, 64], P(('gene', 'cell')), may hold values from -1.5 to 1.5
- cell_offset: float32 [8192], P('cell'), may hold values from -1.2 to 1.2
- gene_offset: float32 [16384], P('gene'), may hold values from -1.2 to 1.2
Outputs:
- new_factors: float32 [8192, 64], P(('cell', 'gene'))
- new_loadings: float32 [16384, 64], P(('gene', 'cell'))
All inputs are finite; a program needn't handle non-finite values.
Results may differ from a plain program's by a relative error of at most 0.0003.
Values sent between devices are 32-bit elements; how exact they have to be, the bound alone decides.
No kernel may reach another device: no remote copies, remote signals or barrier semaphores. Data moves between devices by JAX's collectives and lax.ppermute only.
A program may use at most 128 MiB of HBM per device.

v0:
```python
import jax
import jax.numpy as jnp
from jax import lax
from jax.sharding import PartitionSpec as P

ITERS = 2


epsilon = 1e-06
step_cap = 0.25


def bounded(ratio):
    return step_cap * jnp.tanh(ratio / step_cap)


def predict(factor_rows, loading_rows, cell_part, gene_part, count_part):
    linear = jnp.dot(
        factor_rows,
        loading_rows.T,
        preferred_element_type=jnp.float32,
        precision=lax.Precision.HIGHEST,
    )
    linear = linear + cell_part[:, None] + gene_part[None, :]
    means = jnp.exp(linear)
    excess = means - count_part.astype(jnp.float32)
    return (means, excess)


def per_device(counts, factors, loadings, cell_offset, gene_offset):
    rank = factors.shape[1]
    factor_block = lax.all_gather(factors, "gene", axis=0, tiled=True)
    loading_block = lax.all_gather(loadings, "cell", axis=0, tiled=True)
    own_u = factors
    own_v = loadings
    for iteration in range(ITERS):
        factor_rows = factor_block
        factor_means, factor_excess = predict(
            factor_rows, loading_block, cell_offset, gene_offset, counts
        )
        grad_u = jnp.dot(
            factor_excess,
            loading_block,
            preferred_element_type=jnp.float32,
            precision=lax.Precision.HIGHEST,
        )
        curv_u = jnp.dot(
            factor_means,
            loading_block * loading_block,
            preferred_element_type=jnp.float32,
            precision=lax.Precision.HIGHEST,
        )
        shares = lax.psum_scatter(
            jnp.concatenate([grad_u, curv_u], axis=1), "gene", scatter_dimension=0, tiled=True
        )
        own_u = own_u - bounded(shares[:, :rank] / (shares[:, rank:] + epsilon))
        factor_block = lax.all_gather(own_u, "gene", axis=0, tiled=True)
        loading_rows = loading_block
        means, excess = predict(factor_block, loading_rows, cell_offset, gene_offset, counts)
        contract = (((0,), (0,)), ((), ()))
        grad_v = lax.dot_general(
            excess,
            factor_block,
            contract,
            precision=lax.Precision.HIGHEST,
            preferred_element_type=jnp.float32,
        )
        curv_v = lax.dot_general(
            means,
            factor_block * factor_block,
            contract,
            precision=lax.Precision.HIGHEST,
            preferred_element_type=jnp.float32,
        )
        shares = lax.psum_scatter(
            jnp.concatenate([grad_v, curv_v], axis=1), "cell", scatter_dimension=0, tiled=True
        )
        own_v = own_v - bounded(shares[:, :rank] / (shares[:, rank:] + epsilon))
        if iteration + 1 < ITERS:
            loading_block = lax.all_gather(own_v, "cell", axis=0, tiled=True)
    return (own_u, own_v)


def solution(mesh):
    in_specs = (
        P("cell", "gene"),
        P(("cell", "gene"), None),
        P(("gene", "cell"), None),
        P("cell"),
        P("gene"),
    )
    out_specs = (P(("cell", "gene"), None), P(("gene", "cell"), None))
    return jax.shard_map(
        per_device, mesh=mesh, in_specs=in_specs, out_specs=out_specs, check_vma=False
    )
```

profile of v0, /device:TPU:0, one launch (start us, length us, event | category | flops | bytes accessed | tf_op | source)
XLA Modules:
  0.0 543.3 jit_solution(16086159749187738286)
XLA Ops:
  8.0 7.4 %all_gather.15 = f32[1024,64]{0,1:T(8,128)S(1)} all-gather(f32[256,64]{0,1:T(8,128)} %param.6), channel_id=1, replica_groups=mesh['cell'=8,'gene'=4] {'gene'}, dimensions={0}, use_global_device_ids=true | all-gather | bytes 327680 | tf_op jit(solution)/shard_map/all_gather | solution.py:32
  15.4 37.8 %all-gather.3.cloned.1.call-done = f32[4096,64]{0,1:T(8,128)} async-done(((f32[512,64]{0,1:T(8,128)}), f32[4096,64]{0,1:T(8,128)}) %all-gather.3.cloned.1.call-update) | async-done | bytes 1048592 | tf_op jit(solution)/shard_map/all_gather | solution.py:33
  53.1 15.2 %fusion.56 = f32[1024,4096]{1,0:T(8,128)S(1)} fusion(f32[1024,64]{0,1:T(8,128)S(1)} %all_gather.15, f32[4096,64]{0,1:T(8,128)} %all-gather.3.cloned.1.call-done), kind=kOutput, calls=%fused_computation.68 | convolution fusion | flops 3221225472 | bytes 18087936 | tf_op jit(solution)/shard_map/dot_general | solution.py:18
  68.4 5.7 %copy-done.1 = f32[1024,4096]{1,0:T(8,128)} copy-done((f32[1024,4096]{1,0:T(8,128)}, f32[1024,4096]{1,0:T(8,128)S(1)}, u32[]{:S(2)}) %copy-start.1) | copy-done | bytes 16777240
  74.1 27.7 %fusion.12 = f32[1024,64]{0,1:T(8,128)S(1)} fusion(f32[1024,4096]{1,0:T(8,128)S(1)} %fusion.56, f32[4096]{0:T(1024)S(1)} %copy-done.8, f32[1024]{0:T(1024)S(1)} %copy-done.11, f32[4096,64]{0,1:T(8,128)S(1)} %copy-done.4), kind=kOutput, calls=%fused_computation.16 | convolution fusion | flops 3229876224 | bytes 18108416 | tf_op jit(solution)/shard_map/dot_general | solution.py:47
  101.9 24.1 %fusion.6 = f32[1024,64]{0,1:T(8,128)S(1)} fusion(f32[4096,64]{0,1:T(8,128)S(1)} %copy-done.4, s32[1024,4096]{1,0:T(8,128)} %param.5, f32[1024,4096]{1,0:T(8,128)} %copy-done.1, f32[4096]{0:T(1024)S(1)} %copy-done.8, f32[1024]{0:T(1024)S(1)} %copy-done.11), kind=kOutput, calls=%fused_computation.9 | convolution fusion | flops 3238002688 | bytes 34885632 | tf_op jit(solution)/shard_map/dot_general | solution.py:41
  126.9 20.5 %reduce-scatter.5.cloned.1.call-done = f32[256,128]{0,1:T(8,128)} async-done(((f32[1024,128]{0,1:T(8,128)}), f32[256,128]{0,1:T(8,128)}) %reduce-scatter.5.cloned.1.call-update) | async-done | bytes 131088 | tf_op jit(solution)/shard_map/reduce_scatter | solution.py:53
  148.3 6.2 %all_gather.17 = f32[1024,64]{0,1:T(8,128)S(1)} all-gather(f32[256,64]{0,1:T(8,128)S(1)} %fusion.55), channel_id=1, replica_groups=mesh['cell'=8,'gene'=4] {'gene'}, dimensions={0}, use_global_device_ids=true | all-gather | bytes 327680 | tf_op jit(solution)/shard_map/all_gather | solution.py:57
  154.5 13.8 %fusion.57 = f32[1024,4096]{1,0:T(8,128)S(1)} fusion(f32[1024,64]{0,1:T(8,128)S(1)} %all_gather.17, f32[4096,64]{0,1:T(8,128)S(1)} %copy-done.4), kind=kOutput, calls=%fused_computation.69 | convolution fusion | flops 3221225472 | bytes 18087936 | tf_op jit(solution)/shard_map/dot_general | solution.py:18
  168.4 5.7 %copy-done.2 = f32[1024,4096]{1,0:T(8,128)} copy-done((f32[1024,4096]{1,0:T(8,128)}, f32[1024,4096]{1,0:T(8,128)S(1)}, u32[]{:S(2)}) %copy-start.2) | copy-done | bytes 16777240
  174.1 13.0 %fusion.13 = f32[4096,64]{0,1:T(8,128)S(1)} fusion(f32[1024,4096]{1,0:T(8,128)S(1)} %fusion.57, f32[4096]{0:T(1024)S(1)} %copy-done.8, f32[1024]{0:T(1024)S(1)} %copy-done.11, f32[1024,64]{0,1:T(8,128)S(1)} %all_gather.17), kind=kOutput, calls=%fused_computation.17 | convolution fusion | flops 3229679616 | bytes 18108416 | tf_op jit(solution)/shard_map/dot_general | solution.py:68
  187.1 20.3 %fusion.4 = f32[4096,64]{0,1:T(8,128)S(1)} fusion(f32[1024,64]{0,1:T(8,128)S(1)} %all_gather.17, s32[1024,4096]{1,0:T(8,128)} %param.5, f32[1024,4096]{1,0:T(8,128)} %copy-done.2, f32[4096]{0:T(1024)S(1)} %copy-done.8, f32[1024]{0:T(1024)S(1)} %copy-done.11), kind=kOutput, calls=%fused_computation.6 | convolution fusion | flops 3238002688 | bytes 34885632 | tf_op jit(solution)/shard_map/dot_general | solution.py:61
  209.0 68.2 %reduce-scatter.7.cloned.1.call-done = f32[512,128]{0,1:T(8,128)} async-done(((f32[4096,128]{0,1:T(8,128)}), f32[512,128]{0,1:T(8,128)}) %reduce-scatter.7.cloned.1.call-update) | async-done | bytes 262160 | tf_op jit(solution)/shard_map/reduce_scatter | solution.py:75
  279.4 39.9 %all-gather.5.cloned.1.call-done = f32[4096,64]{0,1:T(8,128)} async-done(((f32[512,64]{0,1:T(8,128)}), f32[4096,64]{0,1:T(8,128)}) %all-gather.5.cloned.1.call-update) | async-done | bytes 1048592 | tf_op jit(solution)/shard_map/all_gather | solution.py:80
  319.3 15.1 %fusion.58 = f32[1024,4096]{1,0:T(8,128)S(1)} fusion(f32[1024,64]{0,1:T(8,128)S(1)} %all_gather.17, f32[4096,64]{0,1:T(8,128)} %all-gather.5.cloned.1.call-done), kind=kOutput, calls=%fused_computation.70 | convolution fusion | flops 3221225472 | bytes 18087936 | tf_op jit(solution)/shard_map/dot_general | solution.py:18
  340.2 18.9 %fusion.14 = f32[1024,64]{0,1:T(8,128)S(1)} fusion(f32[1024,4096]{1,0:T(8,128)S(1)} %fusion.58, f32[4096]{0:T(1024)S(1)} %copy-done.8, f32[1024]{0:T(1024)S(1)} %copy-done.11, f32[4096,64]{0,1:T(8,128)S(1)} %copy-done.5), kind=kOutput, calls=%fused_computation.18 | convolution fusion | flops 3229876224 | bytes 18108416 | tf_op jit(solution)/shard_map/dot_general | solution.py:47
  359.2 24.0 %fusion.2 = f32[1024,64]{0,1:T(8,128)S(1)} fusion(f32[4096,64]{0,1:T(8,128)S(1)} %copy-done.5, s32[1024,4096]{1,0:T(8,128)} %param.5, f32[1024,4096]{1,0:T(8,128)} %copy-done.3, f32[4096]{0:T(1024)S(1)} %copy-done.8, f32[1024]{0:T(1024)S(1)} %copy-done.11), kind=kOutput, calls=%fused_computation.3 | convolution fusion | flops 3238002688 | bytes 34885632 | tf_op jit(solution)/shard_map/dot_general | solution.py:41
  384.1 20.5 %reduce-scatter.9.cloned.1.call-done = f32[256,128]{0,1:T(8,128)} async-done(((f32[1024,128]{0,1:T(8,128)}), f32[256,128]{0,1:T(8,128)}) %reduce-scatter.9.cloned.1.call-update) | async-done | bytes 131088 | tf_op jit(solution)/shard_map/reduce_scatter | solution.py:53
  405.5 6.0 %all_gather.19 = f32[1024,64]{0,1:T(8,128)S(1)} all-gather(f32[256,64]{0,1:T(8,128)S(1)} %fusion.50), channel_id=1, replica_groups=mesh['cell'=8,'gene'=4] {'gene'}, dimensions={0}, use_global_device_ids=true | all-gather | bytes 327680 | tf_op jit(solution)/shard_map/all_gather | solution.py:57
  411.5 13.9 %fusion.59 = f32[1024,4096]{1,0:T(8,128)S(1)} fusion(f32[1024,64]{0,1:T(8,128)S(1)} %all_gather.19, f32[4096,64]{0,1:T(8,128)S(1)} %copy-done.5), kind=kOutput, calls=%fused_computation.71 | convolution fusion | flops 3221225472 | bytes 18087936 | tf_op jit(solution)/shard_map/dot_general | solution.py:18
  425.4 5.7 %copy-done = f32[1024,4096]{1,0:T(8,128)} copy-done((f32[1024,4096]{1,0:T(8,128)}, f32[1024,4096]{1,0:T(8,128)S(1)}, u32[]{:S(2)}) %copy-start) | copy-done | bytes 16777240
  431.1 13.0 %fusion.15 = f32[4096,64]{0,1:T(8,128)S(1)} fusion(f32[1024,4096]{1,0:T(8,128)S(1)} %fusion.59, f32[4096]{0:T(1024)S(1)} %copy-done.8, f32[1024]{0:T(1024)S(1)} %copy-done.11, f32[1024,64]{0,1:T(8,128)S(1)} %all_gather.19), kind=kOutput, calls=%fused_computation.19 | convolution fusion | flops 3229679616 | bytes 18108416 | tf_op jit(solution)/shard_map/dot_general | solution.py:68
  444.2 20.3 %fusion = f32[4096,64]{0,1:T(8,128)S(1)} fusion(f32[1024,64]{0,1:T(8,128)S(1)} %all_gather.19, s32[1024,4096]{1,0:T(8,128)} %param.5, f32[1024,4096]{1,0:T(8,128)} %copy-done, f32[4096]{0:T(1024)S(1)} %copy-done.8, f32[1024]{0:T(1024)S(1)} %copy-done.11), kind=kOutput, calls=%fused_computation | convolution fusion | flops 3238002688 | bytes 34885632 | tf_op jit(solution)/shard_map/dot_general | solution.py:61
  466.1 68.2 %reduce-scatter.11.cloned.1.call-done = f32[512,128]{0,1:T(8,128)} async-done(((f32[4096,128]{0,1:T(8,128)}), f32[512,128]{0,1:T(8,128)}) %reduce-scatter.11.cloned.1.call-update) | async-done | bytes 262160 | tf_op jit(solution)/shard_map/reduce_scatter | solution.py:75
  (41 shorter events, 17.1 us)
Async XLA Ops:
  7.2 67.0 %copy-start.8 = (f32[4096]{0:T(1024)S(1)}, f32[4096]{0:T(1024)}, u32[]{:S(2)}) copy-start(f32[4096]{0:T(1024)} %param.9) | copy-start | bytes 49156
  7.2 67.0 %copy-start.11 = (f32[1024]{0:T(1024)S(1)}, f32[1024]{0:T(1024)}, u32[]{:S(2)}) copy-start(f32[1024]{0:T(1024)} %param.8) | copy-start | bytes 12292
  7.2 45.9 %all-gather.3.cloned.1.call-start = ((), (), s32[]{:S(2)}) async-start(), calls=%async_computation.4 | async-start | bytes 1179648 | tf_op jit(solution)/shard_map/all_gather | solution.py:33
  7.9 139.5 %reduce-scatter.5.cloned.1.call-start = ((), (), s32[]{:S(2)}) async-start(), calls=%async_computation.5 | async-start | bytes 655360 | tf_op jit(solution)/shard_map/reduce_scatter | solution.py:53
  53.1 21.0 %copy-start.4 = (f32[4096,64]{0,1:T(8,128)S(1)}, f32[4096,64]{0,1:T(8,128)}, u32[]{:S(2)}) copy-start(f32[4096,64]{0,1:T(8,128)} %all-gather.3.cloned.1.call-done) | copy-start | bytes 3145732
  68.4 5.7 %copy-start.1 = (f32[1024,4096]{1,0:T(8,128)}, f32[1024,4096]{1,0:T(8,128)S(1)}, u32[]{:S(2)}) copy-start(f32[1024,4096]{1,0:T(8,128)S(1)} %fusion.56) | copy-start | bytes 50331652
  101.9 45.5 %copy-start.9 = (f32[256,64]{0,1:T(8,128)S(1)}, f32[256,64]{0,1:T(8,128)}, u32[]{:S(2)}) copy-start(f32[256,64]{0,1:T(8,128)} %param.6) | copy-start | bytes 196612
  126.8 150.4 %reduce-scatter.7.cloned.1.call-start = ((), (), s32[]{:S(2)}) async-start(), calls=%async_computation.6 | async-start | bytes 2359296 | tf_op jit(solution)/shard_map/reduce_scatter | solution.py:75
  168.4 5.7 %copy-start.2 = (f32[1024,4096]{1,0:T(8,128)}, f32[1024,4096]{1,0:T(8,128)S(1)}, u32[]{:S(2)}) copy-start(f32[1024,4096]{1,0:T(8,128)S(1)} %fusion.57) | copy-start | bytes 50331652
  187.1 90.2 %copy-start.7 = (f32[512,64]{0,1:T(8,128)S(1)}, f32[512,64]{0,1:T(8,128)}, u32[]{:S(2)}) copy-start(f32[512,64]{0,1:T(8,128)} %param.7) | copy-start | bytes 393220
  209.0 110.3 %all-gather.5.cloned.1.call-start = ((), (), s32[]{:S(2)}) async-start(), calls=%async_computation.7 | async-start | bytes 1179648 | tf_op jit(solution)/shard_map/all_gather | solution.py:80
  279.0 125.7 %reduce-scatter.9.cloned.1.call-start = ((), (), s32[]{:S(2)}) async-start(), calls=%async_computation.8 | async-start | bytes 655360 | tf_op jit(solution)/shard_map/reduce_scatter | solution.py:53
  319.3 20.9 %copy-start.5 = (f32[4096,64]{0,1:T(8,128)S(1)}, f32[4096,64]{0,1:T(8,128)}, u32[]{:S(2)}) copy-start(f32[4096,64]{0,1:T(8,128)} %all-gather.5.cloned.1.call-done) | copy-start | bytes 3145732
  334.5 5.7 %copy-start.3 = (f32[1024,4096]{1,0:T(8,128)}, f32[1024,4096]{1,0:T(8,128)S(1)}, u32[]{:S(2)}) copy-start(f32[1024,4096]{1,0:T(8,128)S(1)} %fusion.58) | copy-start | bytes 50331652
  384.1 150.2 %reduce-scatter.11.cloned.1.call-start = ((), (), s32[]{:S(2)}) async-start(), calls=%async_computation.9 | async-start | bytes 2359296 | tf_op jit(solution)/shard_map/reduce_scatter | solution.py:75
  405.5 38.6 %copy-start.10 = (f32[256,64]{0,1:T(8,128)}, f32[256,64]{0,1:T(8,128)S(1)}, u32[]{:S(2)}) copy-start(f32[256,64]{0,1:T(8,128)S(1)} %fusion.50) | copy-start | bytes 196612
  425.4 5.7 %copy-start = (f32[1024,4096]{1,0:T(8,128)}, f32[1024,4096]{1,0:T(8,128)S(1)}, u32[]{:S(2)}) copy-start(f32[1024,4096]{1,0:T(8,128)S(1)} %fusion.59) | copy-start | bytes 50331652
  444.2 90.1 %copy-start.6 = (f32[512,64]{0,1:T(8,128)S(1)}, f32[512,64]{0,1:T(8,128)}, u32[]{:S(2)}) copy-start(f32[512,64]{0,1:T(8,128)} %fusion.45) | copy-start | bytes 393220
Sparse Core Ops, SparseCore 0:
  10.2 42.8 all-gather.2
  127.0 20.4 reduce-scatter.4
  209.1 68.1 reduce-scatter.6
  280.1 39.1 all-gather.4
  384.2 20.3 reduce-scatter.8
  466.2 68.0 reduce-scatter.10
where the time goes:
time: 552 us; the launch traced here: 543 us
  waiting for transfers between devices  256 us (46%)
  matrix products  220 us (40%)
  local copies, waits for them, and re-layouts  23 us (4%)
  blocking collectives  19.6 us (4%)
  between operations  14.7 us (3%)
  other arithmetic  9.9 us (2%)
    reduce_scatter x2, waiting for transfers between devices, per_device(): lax.psum_scatter(jnp.concatenate([grad_v, curv_v], axis=1), 'cell', scatt...  136 us
    dot_general x4, matrix products, predict(): jnp.dot(factor_rows, loading_rows.T, preferred_element_type=jnp.float32,...  58.1 us
    dot_general x2, matrix products, per_device(): jnp.dot(factor_excess, loading_block, preferred_element_type=jnp.float32,...  48.1 us
    dot_general x2, matrix products, per_device(): jnp.dot(factor_means, loading_block * loading_block, preferred_element_ty...  46.7 us
    reduce_scatter x2, waiting for transfers between devices, per_device(): lax.psum_scatter(jnp.concatenate([grad_u, curv_u], axis=1), 'gene', scatt...  41 us
    dot_general x2, matrix products, per_device(): lax.dot_general(excess, factor_block, contract, precision=lax.Precision.H...  40.6 us
    all_gather x1, waiting for transfers between devices, per_device(): loading_block = lax.all_gather(own_v, 'cell', axis=0, tiled=True)  39.9 us
    all_gather x1, waiting for transfers between devices, per_device(): loading_block = lax.all_gather(loadings, 'cell', axis=0, tiled=True)  37.8 us
  transfers between devices with their start and end apart: 6, of which 6 were waited for; matrix products, arithmetic and copies ran while one was open for 0% of the time, Pallas kernels for 0%

commit v1 on v0

v1 whole, which is shorter than its diff:
```python
import functools

import jax
import jax.numpy as jnp
from jax import lax
from jax.experimental import pallas as pl
from jax.experimental.pallas import tpu as pltpu
from jax.sharding import PartitionSpec as P

ITERS = 2
LOG2E = 1.4426950408889634
BF = jnp.bfloat16
F32 = jnp.float32
NT = (((1,), (1,)), ((), ()))

epsilon = 1e-06
step_cap = 0.25


def bounded(ratio):
    return step_cap * jnp.tanh(ratio / step_cap)


def params(megabytes=56):
    return pltpu.CompilerParams(vmem_limit_bytes=megabytes * 2**20)


def pack(rows):
    half = rows.shape[0] // 2
    return jnp.concatenate([rows[:half], rows[half:]], axis=1)


def left_lanes(shape):
    return lax.broadcasted_iota(jnp.int32, shape, 1) < 64


def doubled(packed):
    turned = pltpu.roll(packed, 64, 1)
    left = left_lanes(packed.shape)
    return jnp.concatenate(
        [jnp.where(left, packed, turned), jnp.where(left, turned, packed)], axis=0
    )


def parts(x):
    hi = x.astype(BF).astype(F32)
    return hi, x - hi


def pick(left, a, b):
    return jnp.where(left, a, b).astype(BF)


def queries(x, offset):
    left = left_lanes(x.shape)
    hi, lo = parts(x * LOG2E)
    return jnp.concatenate([pick(left, hi, lo), pick(left, hi, offset.astype(F32))], axis=1)


def keys(x, offset):
    left = left_lanes(x.shape)
    hi, lo = parts(x)
    return jnp.concatenate([hi.astype(BF), pick(left, lo, offset.astype(F32))], axis=1)


def weights(x):
    left = left_lanes(x.shape)
    hi, lo = parts(x)
    square_hi, square_lo = parts(x * x)
    both = jnp.concatenate([pick(left, hi, square_hi), pick(left, lo, square_lo)], axis=1)
    grad = jnp.concatenate([pick(left, -hi, 0.0), pick(left, -lo, 0.0)], axis=1)
    return both, grad


def sums(query, key, weight, count, count_weight):
    linear = lax.dot_general(query, key, NT, preferred_element_type=F32)
    means = jnp.exp2(linear)
    hi = means.astype(BF)
    lo = (means - hi.astype(F32)).astype(BF)
    total = jnp.dot(
        jnp.concatenate([hi, lo, count], axis=1),
        jnp.concatenate([weight, weight, count_weight], axis=0),
        preferred_element_type=F32,
    )
    return total[:, :128] + total[:, 128:]


def offset_columns(offset, is_cell):
    x = offset * LOG2E
    hi = lax.reduce_precision(x, 8, 7)
    mid = lax.reduce_precision(x - hi, 8, 7)
    low = x - hi - mid
    one = jnp.ones_like(x)
    columns = [hi, mid, low, one, one, one] if is_cell else [one, one, one, hi, mid, low]
    stacked = jnp.stack(columns, axis=1).astype(BF)
    return jnp.pad(stacked, ((0, 0), (64, 58)))


def count_kernel(count_ref, plain_ref, turned_ref):
    x = count_ref[...].astype(F32).astype(BF)
    plain_ref[...] = x
    turned_ref[...] = x.T


def count_call(counts, tile=512):
    cells, genes = counts.shape
    return pl.pallas_call(
        count_kernel,
        grid=(genes // tile,),
        in_specs=[pl.BlockSpec((cells, tile), lambda j: (0, j))],
        out_specs=[
            pl.BlockSpec((cells, tile), lambda j: (0, j)),
            pl.BlockSpec((tile, cells), lambda j: (j, 0)),
        ],
        out_shape=[
            jax.ShapeDtypeStruct((cells, genes), BF),
            jax.ShapeDtypeStruct((genes, cells), BF),
        ],
        compiler_params=params(),
        cost_estimate=pl.CostEstimate(flops=0, bytes_accessed=counts.size * 8, transcendentals=0),
    )(counts)


def work(cells, genes):
    return pl.CostEstimate(
        flops=2 * cells * genes * 256 * 4,
        bytes_accessed=2 * cells * genes,
        transcendentals=cells * genes,
    )


def factor_kernel(rows, where, u_ref, cell_ref, mine_ref, other_ref, gene_ref, count_ref, sum_ref, out_ref):
    y = where[1]
    first = jnp.where(y == 0, mine_ref[...], other_ref[...])
    second = jnp.where(y == 0, other_ref[...], mine_ref[...])
    v = jnp.concatenate([doubled(first), doubled(second)], axis=0)
    key = keys(v, gene_ref[...])
    weight, count_weight = weights(v)
    query = queries(doubled(u_ref[...]), cell_ref[...])
    for at in range(0, query.shape[0], rows):
        span = slice(at, at + rows)
        out_ref[span, :] = sum_ref[span, :] + sums(
            query[span], key, weight, count_ref[span, :], count_weight
        )


def factor_call(where, u, cell_columns, mine, other, gene_columns, counts, total, rows=256):
    cells = counts.shape[0]
    half = mine.shape[0]
    tile = 4 * half
    whole = lambda shape: pl.BlockSpec(shape, lambda j, w: (0, 0))
    return pl.pallas_call(
        functools.partial(factor_kernel, rows),
        grid_spec=pltpu.PrefetchScalarGridSpec(
            num_scalar_prefetch=1,
            grid=(1,),
            in_specs=[
                whole(u.shape),
                whole(cell_columns.shape),
                whole(mine.shape),
                whole(other.shape),
                pl.BlockSpec((tile, 128), lambda j, w: (w[0], 0)),
                pl.BlockSpec((cells, tile), lambda j, w: (0, w[0])),
                whole((cells, 128)),
            ],
            out_specs=whole((cells, 128)),
        ),
        out_shape=jax.ShapeDtypeStruct((cells, 128), F32),
        input_output_aliases={7: 0},
        compiler_params=params(),
        cost_estimate=work(cells, tile),
    )(where, u, cell_columns, mine, other, gene_columns, counts, total)


def loading_kernel(rows, where, u_ref, cell_ref, mine_ref, other_ref, gene_ref, turned_ref, mine_out, other_out):
    y = where[1]
    u = doubled(u_ref[...])
    key = keys(u, cell_ref[...])
    weight, count_weight = weights(u)
    count = mine_ref.shape[0] * 2
    for target, v_ref, place in ((other_out, other_ref, 1 - y), (mine_out, mine_ref, y)):
        base = place * count
        query = queries(doubled(v_ref[...]), gene_ref[pl.ds(pl.multiple_of(base, count), count), :])
        for at in range(0, count, rows):
            target[at : at + rows, :] = sums(
                query[at : at + rows],
                key,
                weight,
                turned_ref[pl.ds(pl.multiple_of(base + at, rows), rows), :],
                count_weight,
            )


def loading_call(where, u, cell_columns, mine, other, gene_columns, turned, rows=256):
    cells = turned.shape[1]
    half = mine.shape[0]
    tile = 4 * half
    whole = lambda shape: pl.BlockSpec(shape, lambda j, w: (0, 0))
    return pl.pallas_call(
        functools.partial(loading_kernel, rows),
        grid_spec=pltpu.PrefetchScalarGridSpec(
            num_scalar_prefetch=1,
            grid=(1,),
            in_specs=[
                whole(u.shape),
                whole(cell_columns.shape),
                whole(mine.shape),
                whole(other.shape),
                pl.BlockSpec((tile, 128), lambda j, w: (w[0], 0)),
                pl.BlockSpec((tile, cells), lambda j, w: (w[0], 0)),
            ],
            out_specs=[whole((2 * half, 128))] * 2,
        ),
        out_shape=[jax.ShapeDtypeStruct((2 * half, 128), F32)] * 2,
        compiler_params=params(),
        cost_estimate=work(cells, tile),
    )(where, u, cell_columns, mine, other, gene_columns, turned)


def stepped(packed, total):
    half = packed.shape[0]
    step = bounded(total[:, :64] / (total[:, 64:] + epsilon))
    return packed - jnp.concatenate([step[:half], step[half:]], axis=1)


def swap(x, axis, size, mask):
    return lax.ppermute(x, axis, [(i, i ^ mask) for i in range(size)])


def overlapped(counts, factors, loadings, cell_offset, gene_offset, n_cell, n_gene):
    cell = lax.axis_index("cell")
    gene = lax.axis_index("gene")
    core, x = gene % 2, gene // 2
    y, z = cell % 2, cell // 2
    n_z = n_cell // 2

    def over_cell(value, mask):
        return swap(value, "cell", n_cell, mask)

    def over_gene(value, mask):
        return swap(value, "gene", n_gene, mask)

    def in_order(place, mine, other, axis):
        return jnp.where(
            place == 0,
            jnp.concatenate([mine, other], axis=axis),
            jnp.concatenate([other, mine], axis=axis),
        )

    def gather_loadings(own):
        mine = [own] + [over_cell(own, 2 * s) for s in range(1, n_z)]
        other = [over_cell(m, 1) for m in mine]
        return mine, other

    own_v = pack(loadings)
    v_mine, v_other = gather_loadings(own_v)
    u_half = in_order(x, factors, over_gene(factors, 2), 1)
    u_block = in_order(core, u_half, over_gene(u_half, 1), 0)
    plain, turned = count_call(counts)
    cell_columns = offset_columns(cell_offset, True)
    gene_columns = offset_columns(gene_offset, False)
    where = [jnp.stack([z ^ s, y]) for s in range(n_z)]
    rows = factors.shape[0]

    for iteration in range(ITERS):
        total = jnp.zeros((cell_offset.shape[0], 128), F32)
        for s in range(n_z):
            total = factor_call(
                where[s], u_block, cell_columns, v_mine[s], v_other[s], gene_columns, plain, total
            )
        split = total.reshape(2, 2, rows, 128)
        keep = lax.dynamic_index_in_dim(split, core, 1, False).reshape(2 * rows, 128)
        send = lax.dynamic_index_in_dim(split, 1 - core, 1, False).reshape(2 * rows, 128)
        keep = keep + over_gene(send, 1)
        keep = keep + over_gene(keep, 2)
        u_half = stepped(u_half, keep)
        u_block = in_order(core, u_half, over_gene(u_half, 1), 0)

        shares = [None] * n_z
        for s in [2, 3, 1, 0]:
            mine, other = loading_call(
                where[s], u_block, cell_columns, v_mine[s], v_other[s], gene_columns, turned
            )
            mine = mine + over_cell(other, 1)
            shares[s] = mine if s == 0 else over_cell(mine, 2 * s)
        total = shares[0] + shares[1] + shares[2] + shares[3]
        own_v = stepped(own_v, total)
        if iteration + 1 < ITERS:
            v_mine, v_other = gather_loadings(own_v)

    new_u = jnp.where(x == 0, u_half[:, :64], u_half[:, 64:])
    new_v = jnp.concatenate([own_v[:, :64], own_v[:, 64:]], axis=0)
    return new_u, new_v


def predict(factor_rows, loading_rows, cell_part, gene_part, count_part):
    linear = jnp.dot(
        factor_rows,
        loading_rows.T,
        preferred_element_type=jnp.float32,
        precision=lax.Precision.HIGHEST,
    )
    linear = linear + cell_part[:, None] + gene_part[None, :]
    means = jnp.exp(linear)
    excess = means - count_part.astype(jnp.float32)
    return (means, excess)


def plain_sweeps(counts, factors, loadings, cell_offset, gene_offset):
    rank = factors.shape[1]
    precise = dict(preferred_element_type=F32, precision=lax.Precision.HIGHEST)
    contract = (((0,), (0,)), ((), ()))
    own_u, own_v = factors, loadings
    u = lax.all_gather(own_u, "gene", axis=0, tiled=True)
    v = lax.all_gather(own_v, "cell", axis=0, tiled=True)
    for iteration in range(ITERS):
        means, excess = predict(u, v, cell_offset, gene_offset, counts)
        grad = jnp.dot(excess, v, **precise)
        curv = jnp.dot(means, v * v, **precise)
        shares = lax.psum_scatter(
            jnp.concatenate([grad, curv], axis=1), "gene", scatter_dimension=0, tiled=True
        )
        own_u = own_u - bounded(shares[:, :rank] / (shares[:, rank:] + epsilon))
        u = lax.all_gather(own_u, "gene", axis=0, tiled=True)
        means, excess = predict(u, v, cell_offset, gene_offset, counts)
        grad = lax.dot_general(excess, u, contract, **precise)
        curv = lax.dot_general(means, u * u, contract, **precise)
        shares = lax.psum_scatter(
            jnp.concatenate([grad, curv], axis=1), "cell", scatter_dimension=0, tiled=True
        )
        own_v = own_v - bounded(shares[:, :rank] / (shares[:, rank:] + epsilon))
        if iteration + 1 < ITERS:
            v = lax.all_gather(own_v, "cell", axis=0, tiled=True)
    return own_u, own_v


def solution(mesh):
    n_cell, n_gene = mesh.shape["cell"], mesh.shape["gene"]
    in_specs = (
        P("cell", "gene"),
        P(("cell", "gene"), None),
        P(("gene", "cell"), None),
        P("cell"),
        P("gene"),
    )
    out_specs = (P(("cell", "gene"), None), P(("gene", "cell"), None))
    per_device = plain_sweeps
    if (n_cell, n_gene) == (8, 4):
        per_device = functools.partial(overlapped, n_cell=n_cell, n_gene=n_gene)
    return jax.shard_map(
        per_device, mesh=mesh, in_specs=in_specs, out_specs=out_specs, check_vma=False
    )
```

time: 552 us -> 249 us (0.45)
  matrix products: 220 us -> 0 us
  waiting for transfers between devices: 256 us -> 61.7 us
  Pallas kernels: 0 us -> 113 us
  starting transfers between devices: 0.65 us -> 44.3 us
  blocking collectives: 19.6 us -> 0 us
  between operations: 14.7 us -> 1.31 us
  local copies, waits for them, and re-layouts: 23 us -> 14.6 us
    dot_general x12 -> x0, matrix products: 220 us -> none  [the longest x4 58.1 us: predict(): jnp.dot(factor_rows, loading_rows.T, preferred_element_type=jnp.float32,...]
    reduce_scatter x4 -> x0, waiting for transfers between devices: 177 us -> none  [the longest x2 136 us: per_device(): lax.psum_scatter(jnp.concatenate([grad_v, curv_v], axis=1), 'cell', scatt...]
    pallas_call x0 -> x17, Pallas kernels: none -> 113 us  [the longest x8 50.1 us: factor_call(): pl.pallas_call(functools.partial(factor_kernel, rows), grid_spec=pltpu.Pr...]
    all_gather x2 -> x0, waiting for transfers between devices: 77.7 us -> none  [the longest x1 39.9 us: per_device(): loading_block = lax.all_gather(own_v, 'cell', axis=0, tiled=True)]
    ppermute x0 -> x36, waiting for transfers between devices: none -> 61.7 us  [swap(): return lax.ppermute(x, axis, [(i, i ^ mask) for i in range(size)])]
    ppermute x0 -> x36, starting transfers between devices: none -> 44.3 us  [swap(): return lax.ppermute(x, axis, [(i, i ^ mask) for i in range(size)])]
    all_gather x3 -> x0, blocking collectives: 19.6 us -> none  [the longest x2 12.2 us: per_device(): factor_block = lax.all_gather(own_u, 'gene', axis=0, tiled=True)]
    unnamed x24 -> x51, local copies, waits for them, and re-layouts: 23 us -> 6.52 us
  transfers between devices with their start and end apart: 6 -> 36, of which waited for: 6 -> 15; matrix products, arithmetic and copies ran while one was open for 0% -> 5% of each run, Pallas kernels for 0% -> 36%
where the time goes in v1:
time: 249 us; the launch traced here: 245 us
  Pallas kernels  113 us (45%)
  waiting for transfers between devices  61.7 us (25%)
  starting transfers between devices  44.3 us (18%)
  local copies, waits for them, and re-layouts  14.6 us (6%)
  other arithmetic  9.82 us (4%)
    ppermute x36, waiting for transfers between devices, swap(): return lax.ppermute(x, axis, [(i, i ^ mask) for i in range(size)])  61.7 us
    pallas_call x8, Pallas kernels, factor_call(): pl.pallas_call(functools.partial(factor_kernel, rows), grid_spec=pltpu.Pr...  50.1 us
    pallas_call x8, Pallas kernels, loading_call(): pl.pallas_call(functools.partial(loading_kernel, rows), grid_spec=pltpu.P...  49 us
    ppermute x36, starting transfers between devices, swap(): return lax.ppermute(x, axis, [(i, i ^ mask) for i in range(size)])  44.3 us
    pallas_call x1, Pallas kernels, count_call(): pl.pallas_call(count_kernel, grid=(genes // tile,), in_specs=[pl.BlockSpe...  14.2 us
    unnamed x51, local copies, waits for them, and re-layouts  6.52 us
  transfers between devices with their start and end apart: 36, of which 15 were waited for; matrix products, arithmetic and copies ran while one was open for 5% of the time, Pallas kernels for 36%

profile of v1, /device:TPU:0, one launch (start us, length us, event | category | flops | bytes accessed | tf_op | source)
XLA Modules:
  0.0 245.0 jit_solution(11007383444187115357)
XLA Ops:
  20.0 14.2 %shard_map.68 = (bf16[1024,4096]{1,0:T(8,128)(2,1)}, bf16[4096,1024]{1,0:T(8,128)(2,1)}) custom-call(s32[1024,4096]{1,0:T(8,128)} %count_ref.1), custom_call_target="tpu_custom_call" | custom-call | bytes 33554432 | tf_op jit(solution)/shard_map/pallas_call | solution.py:107
  38.3 6.2 %shard_map.69.sum_ref = f32[1024,128]{1,0:T(8,128)} custom-call(s32[2]{0:T(128)} %pad_add_fusion.3.where, f32[512,128]{1,0:T(8,128)} %maximum_select_fusion.u_ref, bf16[1024,128]{1,0:T(8,128)(2,1)} %pad.8.cell_ref, f32[256,128]{1,0:T(8,128)} %copy-done.2, f32[256,128]{1,0:T(8,128)} %copy-done.3, ...), custom_call_target="tpu_custom_call", output_to_operand_aliasing={{}: (7, {})} | custom-call | flops 2147483648 | bytes 2097152 | tf_op jit(solution)/shard_map/pallas_call | solution.py:152
  45.2 6.2 %shard_map.70.sum_ref = f32[1024,128]{1,0:T(8,128)} custom-call(s32[2]{0:T(128)} %pad_add_fusion.2.where, f32[512,128]{1,0:T(8,128)} %maximum_select_fusion.u_ref, bf16[1024,128]{1,0:T(8,128)(2,1)} %pad.8.cell_ref, f32[256,128]{1,0:T(8,128)} %copy-done.6, f32[256,128]{1,0:T(8,128)} %copy-done.15, ...), custom_call_target="tpu_custom_call", output_to_operand_aliasing={{}: (7, {})} | custom-call | flops 2147483648 | bytes 2097152 | tf_op jit(solution)/shard_map/pallas_call | solution.py:152
  52.0 6.2 %shard_map.71.sum_ref = f32[1024,128]{1,0:T(8,128)} custom-call(s32[2]{0:T(128)} %pad_add_fusion.1.where, f32[512,128]{1,0:T(8,128)} %maximum_select_fusion.u_ref, bf16[1024,128]{1,0:T(8,128)(2,1)} %pad.8.cell_ref, f32[256,128]{1,0:T(8,128)} %copy-done.5, f32[256,128]{1,0:T(8,128)} %copy-done.14, ...), custom_call_target="tpu_custom_call", output_to_operand_aliasing={{}: (7, {})} | custom-call | flops 2147483648 | bytes 2097152 | tf_op jit(solution)/shard_map/pallas_call | solution.py:152
  58.9 6.2 %shard_map.72 = f32[1024,128]{1,0:T(8,128)} custom-call(s32[2]{0:T(128)} %pad_add_fusion.where, f32[512,128]{1,0:T(8,128)} %maximum_select_fusion.u_ref, bf16[1024,128]{1,0:T(8,128)(2,1)} %pad.8.cell_ref, f32[256,128]{1,0:T(8,128)} %copy-done.4, f32[256,128]{1,0:T(8,128)} %copy-done.12, ...), custom_call_target="tpu_custom_call", output_to_operand_aliasing={{}: (7, {})} | custom-call | flops 2147483648 | bytes 2097152 | tf_op jit(solution)/shard_map/pallas_call | solution.py:152
  69.6 6.6 %collective-permute-done.10 = f32[512,128]{1,0:T(8,128)S(1)} collective-permute-done((f32[512,128]{1,0:T(8,128)S(1)}, f32[512,128]{1,0:T(8,128)S(1)}, u32[]{:S(2)}, u32[]{:S(2)}) %collective-permute-start.10) | collective-permute-done | bytes 262176 | tf_op jit(solution)/shard_map/ppermute | solution.py:227
  78.7 6.3 %shard_map.74 = (f32[512,128]{1,0:T(8,128)}, f32[512,128]{1,0:T(8,128)}) custom-call(s32[2]{0:T(128)} %pad_add_fusion.2.where, f32[512,128]{1,0:T(8,128)} %maximum_select_fusion.1.u_ref, bf16[1024,128]{1,0:T(8,128)(2,1)} %pad.8.cell_ref, f32[256,128]{1,0:T(8,128)} %copy-done.6, f32[256,128]{1,0:T(8,128)} %copy-done.15, bf16[4096,128]{1,0:T(8,128)(2,1)} %pad.9.gene_ref, ...), custom_call_target="tpu_custom_call" | custom-call | flops 2147483648 | bytes 2097152 | tf_op jit(solution)/shard_map/pallas_call | solution.py:199
  86.7 6.1 %shard_map.75 = (f32[512,128]{1,0:T(8,128)}, f32[512,128]{1,0:T(8,128)}) custom-call(s32[2]{0:T(128)} %pad_add_fusion.1.where, f32[512,128]{1,0:T(8,128)} %maximum_select_fusion.1.u_ref, bf16[1024,128]{1,0:T(8,128)(2,1)} %pad.8.cell_ref, f32[256,128]{1,0:T(8,128)} %copy-done.5, f32[256,128]{1,0:T(8,128)} %copy-done.14, bf16[4096,128]{1,0:T(8,128)(2,1)} %pad.9.gene_ref, ...), custom_call_target="tpu_custom_call" | custom-call | flops 2147483648 | bytes 2097152 | tf_op jit(solution)/shard_map/pallas_call | solution.py:199
  93.1 6.1 %shard_map.76 = (f32[512,128]{1,0:T(8,128)}, f32[512,128]{1,0:T(8,128)}) custom-call(s32[2]{0:T(128)} %pad_add_fusion.where, f32[512,128]{1,0:T(8,128)} %maximum_select_fusion.1.u_ref, bf16[1024,128]{1,0:T(8,128)(2,1)} %pad.8.cell_ref, f32[256,128]{1,0:T(8,128)} %copy-done.4, f32[256,128]{1,0:T(8,128)} %copy-done.12, bf16[4096,128]{1,0:T(8,128)(2,1)} %pad.9.gene_ref, ...), custom_call_target="tpu_custom_call" | custom-call | flops 2147483648 | bytes 2097152 | tf_op jit(solution)/shard_map/pallas_call | solution.py:199
  101.0 6.1 %shard_map.73 = (f32[512,128]{1,0:T(8,128)}, f32[512,128]{1,0:T(8,128)}) custom-call(s32[2]{0:T(128)} %pad_add_fusion.3.where, f32[512,128]{1,0:T(8,128)} %maximum_select_fusion.1.u_ref, bf16[1024,128]{1,0:T(8,128)(2,1)} %pad.8.cell_ref, f32[256,128]{1,0:T(8,128)} %copy-done.2, f32[256,128]{1,0:T(8,128)} %copy-done.3, bf16[4096,128]{1,0:T(8,128)(2,1)} %pad.9.gene_ref, ...), custom_call_target="tpu_custom_call" | custom-call | flops 2147483648 | bytes 2097152 | tf_op jit(solution)/shard_map/pallas_call | solution.py:199
  114.7 4.5 %collective-permute-done.14 = f32[512,128]{1,0:T(8,128)S(1)} collective-permute-done((f32[512,128]{1,0:T(8,128)S(1)}, f32[512,128]{1,0:T(8,128)S(1)}, u32[]{:S(2)}, u32[]{:S(2)}) %collective-permute-start.14) | collective-permute-done | bytes 262176 | tf_op jit(solution)/shard_map/ppermute | solution.py:227
  119.3 11.1 %collective-permute-done.16 = f32[512,128]{1,0:T(8,128)S(1)} collective-permute-done((f32[512,128]{1,0:T(8,128)S(1)}, f32[512,128]{1,0:T(8,128)S(1)}, u32[]{:S(2)}, u32[]{:S(2)}) %collective-permute-start.16) | collective-permute-done | bytes 262176 | tf_op jit(solution)/shard_map/ppermute | solution.py:227
  141.7 5.5 %collective-permute-done.21.mine_ref = f32[256,128]{1,0:T(8,128)S(1)} collective-permute-done((f32[256,128]{1,0:T(8,128)S(1)}, f32[256,128]{1,0:T(8,128)S(1)}, u32[]{:S(2)}, u32[]{:S(2)}) %collective-permute-start.21) | collective-permute-done | bytes 131104 | tf_op jit(solution)/shard_map/ppermute | solution.py:227
  150.1 6.6 %shard_map.77.sum_ref = f32[1024,128]{1,0:T(8,128)} custom-call(s32[2]{0:T(128)} %pad_add_fusion.3.where, f32[512,128]{1,0:T(8,128)} %maximum_select_fusion.1.u_ref, bf16[1024,128]{1,0:T(8,128)(2,1)} %pad.8.cell_ref, f32[256,128]{1,0:T(8,128)} %copy-done, f32[256,128]{1,0:T(8,128)} %copy-done.7, ...), custom_call_target="tpu_custom_call", output_to_operand_aliasing={{}: (7, {})} | custom-call | flops 2147483648 | bytes 2097152 | tf_op jit(solution)/shard_map/pallas_call | solution.py:152
  157.4 6.2 %shard_map.78.sum_ref = f32[1024,128]{1,0:T(8,128)} custom-call(s32[2]{0:T(128)} %pad_add_fusion.2.where, f32[512,128]{1,0:T(8,128)} %maximum_select_fusion.1.u_ref, bf16[1024,128]{1,0:T(8,128)(2,1)} %pad.8.cell_ref, f32[256,128]{1,0:T(8,128)} %copy-done.10, f32[256,128]{1,0:T(8,128)} %copy-done.16, ...), custom_call_target="tpu_custom_call", output_to_operand_aliasing={{}: (7, {})} | custom-call | flops 2147483648 | bytes 2097152 | tf_op jit(solution)/shard_map/pallas_call | solution.py:152
  164.2 6.2 %shard_map.79.sum_ref = f32[1024,128]{1,0:T(8,128)} custom-call(s32[2]{0:T(128)} %pad_add_fusion.1.where, f32[512,128]{1,0:T(8,128)} %maximum_select_fusion.1.u_ref, bf16[1024,128]{1,0:T(8,128)(2,1)} %pad.8.cell_ref, f32[256,128]{1,0:T(8,128)} %copy-done.9, f32[256,128]{1,0:T(8,128)} %copy-done.13, ...), custom_call_target="tpu_custom_call", output_to_operand_aliasing={{}: (7, {})} | custom-call | flops 2147483648 | bytes 2097152 | tf_op jit(solution)/shard_map/pallas_call | solution.py:152
  171.1 6.2 %shard_map.80 = f32[1024,128]{1,0:T(8,128)} custom-call(s32[2]{0:T(128)} %pad_add_fusion.where, f32[512,128]{1,0:T(8,128)} %maximum_select_fusion.1.u_ref, bf16[1024,128]{1,0:T(8,128)(2,1)} %pad.8.cell_ref, f32[256,128]{1,0:T(8,128)} %copy-done.8, f32[256,128]{1,0:T(8,128)} %copy-done.11, ...), custom_call_target="tpu_custom_call", output_to_operand_aliasing={{}: (7, {})} | custom-call | flops 2147483648 | bytes 2097152 | tf_op jit(solution)/shard_map/pallas_call | solution.py:152
  181.5 6.9 %collective-permute-done.27 = f32[512,128]{1,0:T(8,128)S(1)} collective-permute-done((f32[512,128]{1,0:T(8,128)S(1)}, f32[512,128]{1,0:T(8,128)S(1)}, u32[]{:S(2)}, u32[]{:S(2)}) %collective-permute-start.27) | collective-permute-done | bytes 262176 | tf_op jit(solution)/shard_map/ppermute | solution.py:227
  190.9 6.2 %shard_map.82 = (f32[512,128]{1,0:T(8,128)}, f32[512,128]{1,0:T(8,128)}) custom-call(s32[2]{0:T(128)} %pad_add_fusion.2.where, f32[512,128]{1,0:T(8,128)} %maximum_select_fusion.2.u_ref, bf16[1024,128]{1,0:T(8,128)(2,1)} %pad.8.cell_ref, f32[256,128]{1,0:T(8,128)} %copy-done.10, f32[256,128]{1,0:T(8,128)} %copy-done.16, bf16[4096,128]{1,0:T(8,128)(2,1)} %pad.9.gene_ref, ...), custom_call_target="tpu_custom_call" | custom-call | flops 2147483648 | bytes 2097152 | tf_op jit(solution)/shard_map/pallas_call | solution.py:199
  198.6 6.1 %shard_map.83 = (f32[512,128]{1,0:T(8,128)}, f32[512,128]{1,0:T(8,128)}) custom-call(s32[2]{0:T(128)} %pad_add_fusion.1.where, f32[512,128]{1,0:T(8,128)} %maximum_select_fusion.2.u_ref, bf16[1024,128]{1,0:T(8,128)(2,1)} %pad.8.cell_ref, f32[256,128]{1,0:T(8,128)} %copy-done.9, f32[256,128]{1,0:T(8,128)} %copy-done.13, bf16[4096,128]{1,0:T(8,128)(2,1)} %pad.9.gene_ref, ...), custom_call_target="tpu_custom_call" | custom-call | flops 2147483648 | bytes 2097152 | tf_op jit(solution)/shard_map/pallas_call | solution.py:199
  205.3 6.1 %shard_map.84 = (f32[512,128]{1,0:T(8,128)}, f32[512,128]{1,0:T(8,128)}) custom-call(s32[2]{0:T(128)} %pad_add_fusion.where, f32[512,128]{1,0:T(8,128)} %maximum_select_fusion.2.u_ref, bf16[1024,128]{1,0:T(8,128)(2,1)} %pad.8.cell_ref, f32[256,128]{1,0:T(8,128)} %copy-done.8, f32[256,128]{1,0:T(8,128)} %copy-done.11, bf16[4096,128]{1,0:T(8,128)(2,1)} %pad.9.gene_ref, ...), custom_call_target="tpu_custom_call" | custom-call | flops 2147483648 | bytes 2097152 | tf_op jit(solution)/shard_map/pallas_call | solution.py:199
  212.9 6.1 %shard_map.81 = (f32[512,128]{1,0:T(8,128)}, f32[512,128]{1,0:T(8,128)}) custom-call(s32[2]{0:T(128)} %pad_add_fusion.3.where, f32[512,128]{1,0:T(8,128)} %maximum_select_fusion.2.u_ref, bf16[1024,128]{1,0:T(8,128)(2,1)} %pad.8.cell_ref, f32[256,128]{1,0:T(8,128)} %copy-done, f32[256,128]{1,0:T(8,128)} %copy-done.7, bf16[4096,128]{1,0:T(8,128)(2,1)} %pad.9.gene_ref, ...), custom_call_target="tpu_custom_call" | custom-call | flops 2147483648 | bytes 2097152 | tf_op jit(solution)/shard_map/pallas_call | solution.py:199
  226.7 4.6 %collective-permute-done.31 = f32[512,128]{1,0:T(8,128)S(1)} collective-permute-done((f32[512,128]{1,0:T(8,128)S(1)}, f32[512,128]{1,0:T(8,128)S(1)}, u32[]{:S(2)}, u32[]{:S(2)}) %collective-permute-start.31) | collective-permute-done | bytes 262176 | tf_op jit(solution)/shard_map/ppermute | solution.py:227
  231.3 11.3 %collective-permute-done.33 = f32[512,128]{1,0:T(8,128)S(1)} collective-permute-done((f32[512,128]{1,0:T(8,128)S(1)}, f32[512,128]{1,0:T(8,128)S(1)}, u32[]{:S(2)}, u32[]{:S(2)}) %collective-permute-start.33) | collective-permute-done | bytes 262176 | tf_op jit(solution)/shard_map/ppermute | solution.py:227
  (175 shorter events, 80.0 us)
Async XLA Ops:
  1.8 35.6 %collective-permute-start.8 = (f32[256,128]{1,0:T(8,128)S(1)}, f32[256,128]{1,0:T(8,128)S(1)}, u32[]{:S(2)}, u32[]{:S(2)}) collective-permute-start(f32[256,128]{1,0:T(8,128)S(1)} %pad_maximum_fusion.1.mine_ref), channel_id=1, source_target_pairs={{0,4},{4,0},{8,12},{12,8},{16,20},{20,16},{24,28},{28,24},{1,5},{5... | collective-permute-start | bytes 393224 | tf_op jit(solution)/shard_map/ppermute | solution.py:227
  4.9 29.4 %collective-permute-start.6 = (f32[256,128]{1,0:T(8,128)S(1)}, f32[256,128]{1,0:T(8,128)S(1)}, u32[]{:S(2)}, u32[]{:S(2)}) collective-permute-start(f32[256,128]{1,0:T(8,128)S(1)} %pad_maximum_fusion.1.mine_ref), channel_id=1, source_target_pairs={{0,8},{4,12},{8,0},{12,4},{16,24},{20,28},{24,16},{28,20},{1,9},{5... | collective-permute-start | bytes 393224 | tf_op jit(solution)/shard_map/ppermute | solution.py:227
  6.4 28.2 %collective-permute-start.4 = (f32[256,128]{1,0:T(8,128)S(1)}, f32[256,128]{1,0:T(8,128)S(1)}, u32[]{:S(2)}, u32[]{:S(2)}) collective-permute-start(f32[256,128]{1,0:T(8,128)S(1)} %pad_maximum_fusion.1.mine_ref), channel_id=1, source_target_pairs={{0,16},{4,20},{8,24},{12,28},{16,0},{20,4},{24,8},{28,12},{1,17},{... | collective-permute-start | bytes 393224 | tf_op jit(solution)/shard_map/ppermute | solution.py:227
  9.0 27.4 %collective-permute-start.2 = (f32[256,128]{1,0:T(8,128)S(1)}, f32[256,128]{1,0:T(8,128)S(1)}, u32[]{:S(2)}, u32[]{:S(2)}) collective-permute-start(f32[256,128]{1,0:T(8,128)S(1)} %pad_maximum_fusion.1.mine_ref), channel_id=1, source_target_pairs={{0,24},{4,28},{8,16},{12,20},{16,8},{20,12},{24,0},{28,4},{1,25},{... | collective-permute-start | bytes 393224 | tf_op jit(solution)/shard_map/ppermute | solution.py:227
  15.4 21.4 %collective-permute-start.1 = (f32[256,128]{1,0:T(8,128)S(1)}, f32[256,128]{1,0:T(8,128)S(1)}, u32[]{:S(2)}, u32[]{:S(2)}) collective-permute-start(f32[256,128]{1,0:T(8,128)S(1)} %maximum_select_fusion.3), channel_id=1, source_target_pairs={{0,1},{1,0},{2,3},{3,2},{4,5},{5,4},{6,7},{7,6},{8,9},{9,8},{10,11... | collective-permute-start | bytes 393224 | tf_op jit(solution)/shard_map/ppermute | solution.py:227
  34.7 16.7 %collective-permute-start.5 = (f32[256,128]{1,0:T(8,128)S(1)}, f32[256,128]{1,0:T(8,128)S(1)}, u32[]{:S(2)}, u32[]{:S(2)}) collective-permute-start(f32[256,128]{1,0:T(8,128)S(1)} %collective-permute-done.4.mine_ref), channel_id=1, source_target_pairs={{0,4},{4,0},{8,12},{12,8},{16,20},{20,16},{24,28},{28,24},{1,5},{5... | collective-permute-start | bytes 393224 | tf_op jit(solution)/shard_map/ppermute | solution.py:227
  36.4 21.8 %collective-permute-start.3 = (f32[256,128]{1,0:T(8,128)S(1)}, f32[256,128]{1,0:T(8,128)S(1)}, u32[]{:S(2)}, u32[]{:S(2)}) collective-permute-start(f32[256,128]{1,0:T(8,128)S(1)} %collective-permute-done.2.mine_ref), channel_id=1, source_target_pairs={{0,4},{4,0},{8,12},{12,8},{16,20},{20,16},{24,28},{28,24},{1,5},{5... | collective-permute-start | bytes 393224 | tf_op jit(solution)/shard_map/ppermute | solution.py:227
  85.0 22.3 %collective-permute-start.13 = (f32[512,128]{1,0:T(8,128)}, f32[512,128]{1,0:T(8,128)S(1)}, u32[]{:S(2)}, u32[]{:S(2)}) collective-permute-start(f32[512,128]{1,0:T(8,128)} %get-tuple-element.25), channel_id=1, source_target_pairs={{0,4},{4,0},{8,12},{12,8},{16,20},{20,16},{24,28},{28,24},{1,5},{5... | collective-permute-start | bytes 786440 | tf_op jit(solution)/shard_map/ppermute | solution.py:227
  92.8 15.5 %collective-permute-start.15 = (f32[512,128]{1,0:T(8,128)}, f32[512,128]{1,0:T(8,128)S(1)}, u32[]{:S(2)}, u32[]{:S(2)}) collective-permute-start(f32[512,128]{1,0:T(8,128)} %get-tuple-element.27), channel_id=1, source_target_pairs={{0,4},{4,0},{8,12},{12,8},{16,20},{20,16},{24,28},{28,24},{1,5},{5... | collective-permute-start | bytes 786440 | tf_op jit(solution)/shard_map/ppermute | solution.py:227
  99.2 12.7 %collective-permute-start.17 = (f32[512,128]{1,0:T(8,128)}, f32[512,128]{1,0:T(8,128)S(1)}, u32[]{:S(2)}, u32[]{:S(2)}) collective-permute-start(f32[512,128]{1,0:T(8,128)} %get-tuple-element.29), channel_id=1, source_target_pairs={{0,4},{4,0},{8,12},{12,8},{16,20},{20,16},{24,28},{28,24},{1,5},{5... | collective-permute-start | bytes 786440 | tf_op jit(solution)/shard_map/ppermute | solution.py:227
  107.3 11.9 %collective-permute-start.14 = (f32[512,128]{1,0:T(8,128)S(1)}, f32[512,128]{1,0:T(8,128)S(1)}, u32[]{:S(2)}, u32[]{:S(2)}) collective-permute-start(f32[512,128]{1,0:T(8,128)S(1)} %add.97), channel_id=1, source_target_pairs={{0,8},{4,12},{8,0},{12,4},{16,24},{20,28},{24,16},{28,20},{1,9},{5... | collective-permute-start | bytes 786440 | tf_op jit(solution)/shard_map/ppermute | solution.py:227
  108.4 22.0 %collective-permute-start.16 = (f32[512,128]{1,0:T(8,128)S(1)}, f32[512,128]{1,0:T(8,128)S(1)}, u32[]{:S(2)}, u32[]{:S(2)}) collective-permute-start(f32[512,128]{1,0:T(8,128)S(1)} %add.99), channel_id=1, source_target_pairs={{0,16},{4,20},{8,24},{12,28},{16,0},{20,4},{24,8},{28,12},{1,17},{... | collective-permute-start | bytes 786440 | tf_op jit(solution)/shard_map/ppermute | solution.py:227
  111.9 18.4 %collective-permute-start.18 = (f32[512,128]{1,0:T(8,128)S(1)}, f32[512,128]{1,0:T(8,128)S(1)}, u32[]{:S(2)}, u32[]{:S(2)}) collective-permute-start(f32[512,128]{1,0:T(8,128)S(1)} %add.101), channel_id=1, source_target_pairs={{0,24},{4,28},{8,16},{12,20},{16,8},{20,12},{24,0},{28,4},{1,25},{... | collective-permute-start | bytes 786440 | tf_op jit(solution)/shard_map/ppermute | solution.py:227
  136.0 11.2 %collective-permute-start.21 = (f32[256,128]{1,0:T(8,128)S(1)}, f32[256,128]{1,0:T(8,128)S(1)}, u32[]{:S(2)}, u32[]{:S(2)}) collective-permute-start(f32[256,128]{1,0:T(8,128)S(1)} %maximum_subtract_fusion.1.mine_ref), channel_id=1, source_target_pairs={{0,16},{4,20},{8,24},{12,28},{16,0},{20,4},{24,8},{28,12},{1,17},{... | collective-permute-start | bytes 393224 | tf_op jit(solution)/shard_map/ppermute | solution.py:227
  137.0 11.7 %collective-permute-start.19 = (f32[256,128]{1,0:T(8,128)S(1)}, f32[256,128]{1,0:T(8,128)S(1)}, u32[]{:S(2)}, u32[]{:S(2)}) collective-permute-start(f32[256,128]{1,0:T(8,128)S(1)} %maximum_subtract_fusion.1.mine_ref), channel_id=1, source_target_pairs={{0,24},{4,28},{8,16},{12,20},{16,8},{20,12},{24,0},{28,4},{1,25},{... | collective-permute-start | bytes 393224 | tf_op jit(solution)/shard_map/ppermute | solution.py:227
  140.2 16.5 %collective-permute-start.24 = (f32[256,128]{1,0:T(8,128)S(1)}, f32[256,128]{1,0:T(8,128)S(1)}, u32[]{:S(2)}, u32[]{:S(2)}) collective-permute-start(f32[256,128]{1,0:T(8,128)S(1)} %collective-permute-done.23.mine_ref), channel_id=1, source_target_pairs={{0,4},{4,0},{8,12},{12,8},{16,20},{20,16},{24,28},{28,24},{1,5},{5... | collective-permute-start | bytes 393224 | tf_op jit(solution)/shard_map/ppermute | solution.py:227
  147.2 16.4 %collective-permute-start.22 = (f32[256,128]{1,0:T(8,128)S(1)}, f32[256,128]{1,0:T(8,128)S(1)}, u32[]{:S(2)}, u32[]{:S(2)}) collective-permute-start(f32[256,128]{1,0:T(8,128)S(1)} %collective-permute-done.21.mine_ref), channel_id=1, source_target_pairs={{0,4},{4,0},{8,12},{12,8},{16,20},{20,16},{24,28},{28,24},{1,5},{5... | collective-permute-start | bytes 393224 | tf_op jit(solution)/shard_map/ppermute | solution.py:227
  148.7 21.7 %collective-permute-start.20 = (f32[256,128]{1,0:T(8,128)S(1)}, f32[256,128]{1,0:T(8,128)S(1)}, u32[]{:S(2)}, u32[]{:S(2)}) collective-permute-start(f32[256,128]{1,0:T(8,128)S(1)} %collective-permute-done.19.mine_ref), channel_id=1, source_target_pairs={{0,4},{4,0},{8,12},{12,8},{16,20},{20,16},{24,28},{28,24},{1,5},{5... | collective-permute-start | bytes 393224 | tf_op jit(solution)/shard_map/ppermute | solution.py:227
  197.1 22.4 %collective-permute-start.30 = (f32[512,128]{1,0:T(8,128)}, f32[512,128]{1,0:T(8,128)S(1)}, u32[]{:S(2)}, u32[]{:S(2)}) collective-permute-start(f32[512,128]{1,0:T(8,128)} %get-tuple-element.33), channel_id=1, source_target_pairs={{0,4},{4,0},{8,12},{12,8},{16,20},{20,16},{24,28},{28,24},{1,5},{5... | collective-permute-start | bytes 786440 | tf_op jit(solution)/shard_map/ppermute | solution.py:227
  204.7 16.4 %collective-permute-start.32 = (f32[512,128]{1,0:T(8,128)}, f32[512,128]{1,0:T(8,128)S(1)}, u32[]{:S(2)}, u32[]{:S(2)}) collective-permute-start(f32[512,128]{1,0:T(8,128)} %get-tuple-element.35), channel_id=1, source_target_pairs={{0,4},{4,0},{8,12},{12,8},{16,20},{20,16},{24,28},{28,24},{1,5},{5... | collective-permute-start | bytes 786440 | tf_op jit(solution)/shard_map/ppermute | solution.py:227
  211.3 11.0 %collective-permute-start.34 = (f32[512,128]{1,0:T(8,128)}, f32[512,128]{1,0:T(8,128)S(1)}, u32[]{:S(2)}, u32[]{:S(2)}) collective-permute-start(f32[512,128]{1,0:T(8,128)} %get-tuple-element.37), channel_id=1, source_target_pairs={{0,4},{4,0},{8,12},{12,8},{16,20},{20,16},{24,28},{28,24},{1,5},{5... | collective-permute-start | bytes 786440 | tf_op jit(solution)/shard_map/ppermute | solution.py:227
  219.5 11.7 %collective-permute-start.31 = (f32[512,128]{1,0:T(8,128)S(1)}, f32[512,128]{1,0:T(8,128)S(1)}, u32[]{:S(2)}, u32[]{:S(2)}) collective-permute-start(f32[512,128]{1,0:T(8,128)S(1)} %add.108), channel_id=1, source_target_pairs={{0,8},{4,12},{8,0},{12,4},{16,24},{20,28},{24,16},{28,20},{1,9},{5... | collective-permute-start | bytes 786440 | tf_op jit(solution)/shard_map/ppermute | solution.py:227
  221.1 21.4 %collective-permute-start.33 = (f32[512,128]{1,0:T(8,128)S(1)}, f32[512,128]{1,0:T(8,128)S(1)}, u32[]{:S(2)}, u32[]{:S(2)}) collective-permute-start(f32[512,128]{1,0:T(8,128)S(1)} %add.110), channel_id=1, source_target_pairs={{0,16},{4,20},{8,24},{12,28},{16,0},{20,4},{24,8},{28,12},{1,17},{... | collective-permute-start | bytes 786440 | tf_op jit(solution)/shard_map/ppermute | solution.py:227
  222.4 20.2 %collective-permute-start.35 = (f32[512,128]{1,0:T(8,128)S(1)}, f32[512,128]{1,0:T(8,128)S(1)}, u32[]{:S(2)}, u32[]{:S(2)}) collective-permute-start(f32[512,128]{1,0:T(8,128)S(1)} %add.112), channel_id=1, source_target_pairs={{0,24},{4,28},{8,16},{12,20},{16,8},{20,12},{24,0},{28,4},{1,25},{... | collective-permute-start | bytes 786440 | tf_op jit(solution)/shard_map/ppermute | solution.py:227
  (35 other events, 336.3 us)
